TPU v7x, 32 devices: a whole 2x2x4 slice. The times are simulated.
32 devices in a mesh: groups: 2 (over y), train: 4 (over x, core), proj: 4 (over z).
Axes of the slice: x: 2, y: 2, z: 4, core: 2. Of those that a mesh axis runs over, the one named last changes fastest.
Arguments:
- train_grads: bfloat16 [8192, 16384], P(('groups', 'train'), 'proj'), parts along dimension 0, may hold values from -6 to 6
- queries: bfloat16 [4096, 16384], P(('groups', 'train'), 'proj'), parts along dimension 0, may hold values from -6 to 6
- fisher: float32 [32768], P(('groups', 'proj')), parts along dimension 0, may hold values from 0.25 to 4
- block_pick: int32 [8, 4], P('groups'), parts along dimension 0, may hold values from 0 to 1
Outputs:
- scores: float32 [4, 8192, 256], P(None, ('groups', 'train', 'proj')), parts along dimension 1
There are 2 independent parts, one for each index of `groups`. A program takes and returns all parts, laid end to end along the dimension named above; each array names one. Nothing has to cross between parts.
All inputs are finite; a program needn't handle non-finite values.
Results may differ from a plain program's by a relative error of at most 0.0029.
Values may be sent and summed in bfloat16 or wider, within the bound.
A program may use at most 128 MiB of HBM per device.

v0:
```python
import jax
import jax.numpy as jnp
from jax import lax
from jax.sharding import PartitionSpec as P

P_SIZE = 16384
QB = 256
QBLK = 2
STEPS = 4


def shifted(array, axis, by):
    size = lax.axis_size(axis)
    return lax.ppermute(array, axis, [(i, (i + by) % size) for i in range(size)])


def on_device(train_grads, queries, fisher, block_pick):
    here = lax.axis_index("train")
    width = queries.shape[1]
    precond = (queries.astype(jnp.float32) * lax.rsqrt(fisher)[None, :]).astype(jnp.bfloat16)
    pool = precond.reshape(QBLK, QB, width)
    picks = lax.dynamic_index_in_dim(block_pick, here, 1, keepdims=False)
    own_blocks = [
        lax.dynamic_index_in_dim(pool, picks[step], 0, keepdims=False) for step in range(STEPS)
    ]
    held = [own_blocks[0]]
    pending = jnp.stack(own_blocks[1:])
    for step in range(1, STEPS):
        pending = shifted(pending, "train", 1)
        held.append(pending[0])
        pending = pending[1:]
    scale = P_SIZE ** (-0.5)
    outputs = []
    for step in range(STEPS):
        current = held[step]
        summed = lax.psum_scatter(
            lax.dot_general(
                train_grads, current, (((1,), (1,)), ((), ())), preferred_element_type=jnp.float32
            ),
            "proj",
            scatter_dimension=0,
            tiled=True,
        )
        outputs.append(summed * scale)
    return jnp.stack(outputs)


def solution(mesh):
    placed = (
        P(("groups", "train"), "proj"),
        P(("groups", "train"), "proj"),
        P(("groups", "proj")),
        P("groups", None),
    )
    return jax.shard_map(
        on_device,
        mesh=mesh,
        in_specs=placed,
        out_specs=P(None, ("groups", "train", "proj"), None),
        check_vma=False,
    )
```

profile of v0, /device:TPU:1, one launch (start us, length us, event | category | flops | bytes accessed | tf_op | source)
XLA Modules:
  0.0 226.9 jit_solution(12639218969204094412)
XLA Ops:
  6.5 0.7 copy-done
  7.2 0.1 constant_dynamic-slice_fusion.3
  7.3 0.6 fusion.16
  11.8 0.7 rsqrt.3
  14.4 3.3 %multiply_convert_fusion = bf16[512,4096]{1,0:T(8,128)(2,1)S(1)} fusion(bf16[512,4096]{1,0:T(8,128)(2,1)} %param.5, f32[4096]{0:T(1024)S(1)} %rsqrt.3), kind=kLoop, calls=%fused_computation | loop fusion | flops 6291456 | bytes 8404992 | tf_op jit(solution)/shard_map/convert_element_type | solution.py:20
  17.7 0.8 constant_dynamic-slice_fusion.2
  18.5 1.2 copy-done.1
  19.8 0.8 pad_maximum_fusion
  20.6 2.7 %collective-permute-start = (bf16[3,256,4096]{2,1,0:T(8,128)(2,1)S(1)}, bf16[3,256,4096]{2,1,0:T(8,128)(2,1)S(1)}, u32[]{:S(2)}, u32[]{:S(2)}) collective-permute-start(bf16[3,256,4096]{2,1,0:T(8,128)(2,1)S(1)} %pad_maximum_fusion), channel_id=1, source_target_pairs={{0,4},{4,8},{8,12},{12,0},{1,5},{5,9},{9,13},{13,1},{2,6},{6,10},{... | collective-permute-start | bytes 18874376 | tf_op jit(solution)/shard_map/ppermute | solution.py:14
  23.3 67.9 %collective-permute-done = bf16[3,256,4096]{2,1,0:T(8,128)(2,1)S(1)} collective-permute-done((bf16[3,256,4096]{2,1,0:T(8,128)(2,1)S(1)}, bf16[3,256,4096]{2,1,0:T(8,128)(2,1)S(1)}, u32[]{:S(2)}, u32[]{:S(2)}) %collective-permute-start) | collective-permute-done | bytes 6291488 | tf_op jit(solution)/shard_map/ppermute | solution.py:14
  91.2 2.6 %slice.37 = bf16[2,256,4096]{2,1,0:T(8,128)(2,1)} slice(bf16[3,256,4096]{2,1,0:T(8,128)(2,1)S(1)} %collective-permute-done), slice={[1:3], [0:256], [0:4096]} | slice | bytes 8388608 | tf_op jit(solution)/shard_map/slice | solution.py:31
  93.7 2.5 %collective-permute-start.1 = (bf16[2,256,4096]{2,1,0:T(8,128)(2,1)}, bf16[2,256,4096]{2,1,0:T(8,128)(2,1)}, u32[]{:S(2)}, u32[]{:S(2)}) collective-permute-start(bf16[2,256,4096]{2,1,0:T(8,128)(2,1)} %slice.37), channel_id=1, source_target_pairs={{0,4},{4,8},{8,12},{12,0},{1,5},{5,9},{9,13},{13,1},{2,6},{6,10},{... | collective-permute-start | bytes 12582920 | tf_op jit(solution)/shard_map/ppermute | solution.py:14
  98.2 7.4 %fusion.7 = f32[1024,256]{0,1:T(8,128)} fusion(bf16[1024,4096]{1,0:T(8,128)(2,1)} %param.4, bf16[2,256,4096]{2,1,0:T(8,128)(2,1)} %bitcast.46, s32[]{:T(128)S(6)} %select_n.18), kind=kOutput, calls=%fused_computation.11 | convolution fusion | flops 2147483648 | bytes 11534340 | tf_op jit(solution)/shard_map/dot_general | solution.py:37
  105.6 0.0 reduce-scatter.7.cloned.1.call-start
  105.6 7.4 %fusion.13 = f32[1024,256]{0,1:T(8,128)} fusion(bf16[1024,4096]{1,0:T(8,128)(2,1)} %param.4, bf16[3,256,4096]{2,1,0:T(8,128)(2,1)} %copy-done.2), kind=kOutput, calls=%fused_computation.13 | convolution fusion | flops 2147483648 | bytes 11534336 | tf_op jit(solution)/shard_map/dot_general | solution.py:37
  113.0 0.0 reduce-scatter.9.cloned.1.call-start
  113.1 28.9 %collective-permute-done.1 = bf16[2,256,4096]{2,1,0:T(8,128)(2,1)} collective-permute-done((bf16[2,256,4096]{2,1,0:T(8,128)(2,1)}, bf16[2,256,4096]{2,1,0:T(8,128)(2,1)}, u32[]{:S(2)}, u32[]{:S(2)}) %collective-permute-start.1) | collective-permute-done | bytes 4194336 | tf_op jit(solution)/shard_map/ppermute | solution.py:14
  142.0 1.7 slice.39
  143.7 2.5 %collective-permute-start.2 = (bf16[1,256,4096]{2,1,0:T(8,128)(2,1)S(1)}, bf16[1,256,4096]{2,1,0:T(8,128)(2,1)}, u32[]{:S(2)}, u32[]{:S(2)}) collective-permute-start(bf16[1,256,4096]{2,1,0:T(8,128)(2,1)S(1)} %slice.39), channel_id=1, source_target_pairs={{0,4},{4,8},{8,12},{12,0},{1,5},{5,9},{9,13},{13,1},{2,6},{6,10},{... | collective-permute-start | bytes 6291464 | tf_op jit(solution)/shard_map/ppermute | solution.py:14
  146.2 7.4 %fusion.14 = f32[1024,256]{0,1:T(8,128)} fusion(bf16[1024,4096]{1,0:T(8,128)(2,1)} %param.4, bf16[2,256,4096]{2,1,0:T(8,128)(2,1)} %collective-permute-done.1), kind=kOutput, calls=%fused_computation.14 | convolution fusion | flops 2147483648 | bytes 11534336 | tf_op jit(solution)/shard_map/dot_general | solution.py:37
  153.7 0.2 reduce-scatter.11.cloned.1.call-start
  153.9 15.3 %collective-permute-done.2 = bf16[1,256,4096]{2,1,0:T(8,128)(2,1)} collective-permute-done((bf16[1,256,4096]{2,1,0:T(8,128)(2,1)S(1)}, bf16[1,256,4096]{2,1,0:T(8,128)(2,1)}, u32[]{:S(2)}, u32[]{:S(2)}) %collective-permute-start.2) | collective-permute-done | bytes 2097184 | tf_op jit(solution)/shard_map/ppermute | solution.py:14
  169.2 7.4 %fusion.10 = f32[1024,256]{0,1:T(8,128)} fusion(bf16[1024,4096]{1,0:T(8,128)(2,1)} %param.4, bf16[1,256,4096]{2,1,0:T(8,128)(2,1)} %collective-permute-done.2), kind=kOutput, calls=%fused_computation.12 | convolution fusion | flops 2147483648 | bytes 11534336 | tf_op jit(solution)/shard_map/dot_general | solution.py:37
  176.6 0.0 reduce-scatter.5.cloned.1.call-done
  176.6 1.0 multiply_bitcast_fusion.3
  177.7 1.0 multiply_bitcast_fusion.2
  178.6 11.3 %reduce-scatter.9.cloned.1.call-done = f32[256,256]{0,1:T(8,128)} async-done(((f32[1024,256]{0,1:T(8,128)}), f32[256,256]{0,1:T(8,128)}) %reduce-scatter.9.cloned.1.call-update) | async-done | bytes 262160 | tf_op jit(solution)/shard_map/reduce_scatter | solution.py:36
  189.9 1.0 multiply_bitcast_fusion.1
  190.9 27.1 %reduce-scatter.11.cloned.1.call-done = f32[256,256]{0,1:T(8,128)} async-done(((f32[1024,256]{0,1:T(8,128)}), f32[256,256]{0,1:T(8,128)}) %reduce-scatter.11.cloned.1.call-update) | async-done | bytes 262160 | tf_op jit(solution)/shard_map/reduce_scatter | solution.py:36
  218.0 1.0 multiply_bitcast_fusion
  218.9 0.1 pad_maximum_fusion.1
  219.0 1.3 copy.5
  (10 shorter events, 0.1 us)
Async XLA Ops:
  6.5 0.7 copy-start
  6.5 170.1 %reduce-scatter.5.cloned.1.call-start = ((), (), s32[]{:S(2)}) async-start(), calls=%async_computation.4 | async-start | bytes 1310720 | tf_op jit(solution)/shard_map/reduce_scatter | solution.py:36
  17.7 2.1 copy-start.1
  20.6 70.6 %collective-permute-start = (bf16[3,256,4096]{2,1,0:T(8,128)(2,1)S(1)}, bf16[3,256,4096]{2,1,0:T(8,128)(2,1)S(1)}, u32[]{:S(2)}, u32[]{:S(2)}) collective-permute-start(bf16[3,256,4096]{2,1,0:T(8,128)(2,1)S(1)} %pad_maximum_fusion), channel_id=1, source_target_pairs={{0,4},{4,8},{8,12},{12,0},{1,5},{5,9},{9,13},{13,1},{2,6},{6,10},{... | collective-permute-start | bytes 18874376 | tf_op jit(solution)/shard_map/ppermute | solution.py:14
  91.2 5.0 %copy-start.2 = (bf16[3,256,4096]{2,1,0:T(8,128)(2,1)}, bf16[3,256,4096]{2,1,0:T(8,128)(2,1)S(1)}, u32[]{:S(2)}) copy-start(bf16[3,256,4096]{2,1,0:T(8,128)(2,1)S(1)} %collective-permute-done) | copy-start | bytes 18874372
  93.7 48.2 %collective-permute-start.1 = (bf16[2,256,4096]{2,1,0:T(8,128)(2,1)}, bf16[2,256,4096]{2,1,0:T(8,128)(2,1)}, u32[]{:S(2)}, u32[]{:S(2)}) collective-permute-start(bf16[2,256,4096]{2,1,0:T(8,128)(2,1)} %slice.37), channel_id=1, source_target_pairs={{0,4},{4,8},{8,12},{12,0},{1,5},{5,9},{9,13},{13,1},{2,6},{6,10},{... | collective-permute-start | bytes 12582920 | tf_op jit(solution)/shard_map/ppermute | solution.py:14
  105.6 72.1 %reduce-scatter.7.cloned.1.call-start = ((), (), s32[]{:S(2)}) async-start(), calls=%async_computation.5 | async-start | bytes 1310720 | tf_op jit(solution)/shard_map/reduce_scatter | solution.py:36
  113.0 76.9 %reduce-scatter.9.cloned.1.call-start = ((), (), s32[]{:S(2)}) async-start(), calls=%async_computation.6 | async-start | bytes 1310720 | tf_op jit(solution)/shard_map/reduce_scatter | solution.py:36
  143.7 25.5 %collective-permute-start.2 = (bf16[1,256,4096]{2,1,0:T(8,128)(2,1)S(1)}, bf16[1,256,4096]{2,1,0:T(8,128)(2,1)}, u32[]{:S(2)}, u32[]{:S(2)}) collective-permute-start(bf16[1,256,4096]{2,1,0:T(8,128)(2,1)S(1)} %slice.39), channel_id=1, source_target_pairs={{0,4},{4,8},{8,12},{12,0},{1,5},{5,9},{9,13},{13,1},{2,6},{6,10},{... | collective-permute-start | bytes 6291464 | tf_op jit(solution)/shard_map/ppermute | solution.py:14
  153.7 64.3 %reduce-scatter.11.cloned.1.call-start = ((), (), s32[]{:S(2)}) async-start(), calls=%async_computation.7 | async-start | bytes 1310720 | tf_op jit(solution)/shard_map/reduce_scatter | solution.py:36
Sparse Core Ops, SparseCore 0:
  105.7 27.8 reduce-scatter.4
  135.9 25.7 reduce-scatter.6
  164.1 25.7 reduce-scatter.8
  192.1 25.7 reduce-scatter.10
where the time goes:
time: 228 us; the launch traced here: 227 us
  waiting for transfers between devices  151 us (66%)
  matrix products  29.5 us (13%)
  between operations  21 us (9%)
  local copies, waits for them, and re-layouts  9.71 us (4%)
  other arithmetic  8.04 us (4%)
  starting transfers between devices  7.97 us (3%)
    ppermute x3, waiting for transfers between devices, shifted(): lax.ppermute(array, axis, [(i, (i + by) % size) for i in range(size)])  112 us
    reduce_scatter x4, waiting for transfers between devices, on_device(): lax.psum_scatter(lax.dot_general(train_grads, current, (((1,), (1,)), (()...  38.4 us
    dot_general x4, matrix products, on_device(): lax.dot_general(train_grads, current, (((1,), (1,)), ((), ())), preferred...  29.5 us
    ppermute x3, starting transfers between devices, shifted(): lax.ppermute(array, axis, [(i, (i + by) % size) for i in range(size)])  7.66 us
  transfers between devices with their start and end apart: 7, of which 5 were waited for; matrix products, arithmetic and copies ran while one was open for 15% of the time, Pallas kernels for 0%

commit v1 on v0

v1 whole, which is shorter than its diff:
```python
import functools

import jax
import jax.numpy as jnp
from jax import lax
from jax.experimental import pallas as pl
from jax.experimental.pallas import tpu as pltpu
from jax.sharding import PartitionSpec as P

P_SIZE = 16384
QB = 256
QBLK = 2
STEPS = 4
CHUNK = 64
NCHUNK = QB // CHUNK
MESH = pl.DeviceIdType.MESH


def kernel(
    n_train, n_proj, train_hbm, pool_hbm, fisher, pick, out,
    train, pools, inv_root, outgoing, block, partial, own, landed,
    train_sem, pool_sem, send_sem, recv_sem, zsend_sem, zrecv_sem,
):
    here, z = lax.axis_index("train"), lax.axis_index("proj")
    core = lax.rem(here, 2)
    rows, width = train.shape
    owned = rows // n_proj
    scale = P_SIZE ** (-0.5)

    pool_copies = []
    for c in range(NCHUNK):
        part = pl.ds(c * CHUNK, CHUNK)
        copy = pltpu.make_async_copy(pool_hbm.at[:, part], pools[c], pool_sem.at[c])
        copy.start()
        pool_copies.append(copy)
    train_copy = pltpu.make_async_copy(train_hbm, train, train_sem)
    train_copy.start()

    barrier = pltpu.get_barrier_semaphore()
    for step in range(1, STEPS):
        source = lax.rem(here - step + n_train, n_train)
        pl.semaphore_signal(barrier, inc=1, device_id={"train": source}, device_id_type=MESH)
    for d in range(1, n_proj):
        pl.semaphore_signal(
            barrier, inc=1, device_id={"proj": lax.rem(z - d + n_proj, n_proj)}, device_id_type=MESH
        )
    inv_root[...] = lax.rsqrt(fisher[...])

    def query_copy(step, c):
        part = pl.ds(c * CHUNK, CHUNK)
        return pltpu.make_async_remote_copy(
            src_ref=outgoing.at[step - 1, part],
            dst_ref=block.at[step, part],
            send_sem=send_sem.at[step - 1, c],
            recv_sem=recv_sem.at[step - 1, c],
            device_id={"train": lax.rem(here + step, n_train)},
            device_id_type=MESH,
        )

    def condition(step, c, target, slot):
        chosen = pick[step, here]
        piece = min(width, 512)

        def body(i, _):
            source = pl.ds(pl.multiple_of(i * 16, 16), 16)
            part = pl.ds(pl.multiple_of(c * CHUNK + i * 16, 16), 16)
            for at in range(0, width, piece):
                lanes = pl.ds(at, piece)
                value = pools[c][chosen, source, lanes].astype(jnp.float32) * inv_root[:, lanes]
                target[slot, part, lanes] = value.astype(jnp.bfloat16)
            return 0

        lax.fori_loop(0, CHUNK // 16, body, 0)

    far = (2 - core, 3 - core)
    near = 1 + 2 * core
    for c in range(NCHUNK):
        pool_copies[c].wait()
        for i, step in enumerate((*far, near)):
            condition(step, c, outgoing, step - 1)
            if c == 0 and i == 0:
                pl.semaphore_wait(barrier, STEPS - 1 + n_proj - 1)
            query_copy(step, c).start()
    for c in range(NCHUNK):
        condition(0, c, block, 0)
    train_copy.wait()

    def partial_copy(k, d):
        to = lax.rem(z + d, n_proj)
        return pltpu.make_async_remote_copy(
            src_ref=partial.at[k, pl.ds(pl.multiple_of(to * owned, 16), owned)],
            dst_ref=landed.at[k, d - 1],
            send_sem=zsend_sem.at[k, d - 1],
            recv_sem=zrecv_sem.at[k, d - 1],
            device_id={"proj": to},
            device_id_type=MESH,
        )

    def finish(k, streams, c):
        def add(d, total):
            partial_copy(k, d).wait_recv()
            return total + landed[k, d - 1].astype(jnp.float32)

        total = lax.fori_loop(1, n_proj, add, own[k]) * scale
        for i, step in enumerate(streams):
            out[step, :, c * CHUNK:(c + 1) * CHUNK] = total[:, i * CHUNK:(i + 1) * CHUNK]

    near_in = 3 - 2 * core
    far_in = (1 + core, 2 + core)
    work = [((0, near_in), c) for c in range(NCHUNK)] + [(far_in, c) for c in range(NCHUNK)]
    for k, (streams, c) in enumerate(work):
        part = slice(c * CHUNK, (c + 1) * CHUNK)
        for step in streams:
            if not (isinstance(step, int) and step == 0):
                query_copy(step, c).wait_recv()

        def multiply(d, _):
            to = lax.rem(z + d, n_proj)
            mine = pl.ds(pl.multiple_of(to * owned, 16), owned)
            both = jnp.concatenate([block[step, part] for step in streams], axis=0)
            sums = lax.dot_general(
                train[mine], both, (((1,), (1,)), ((), ())), preferred_element_type=jnp.float32
            )

            @pl.when(d < n_proj)
            def _():
                partial[k, mine] = sums.astype(jnp.bfloat16)
                partial_copy(k, d).start()

            @pl.when(d == n_proj)
            def _():
                own[k] = sums

            return 0

        lax.fori_loop(1, n_proj + 1, multiply, 0)
        if k > 0:
            finish(k - 1, *work[k - 1])
    finish(len(work) - 1, *work[-1])

    for step in range(1, STEPS):
        for c in range(NCHUNK):
            query_copy(step, c).wait_send()
    for k in range(len(work)):
        def drain(d, _):
            partial_copy(k, d).wait_send()
            return 0

        lax.fori_loop(1, n_proj, drain, 0)


def on_device(n_train, n_proj, train_grads, queries, fisher, block_pick):
    rows, width = train_grads.shape
    owned = rows // n_proj
    works = 2 * NCHUNK
    bf16, f32 = jnp.bfloat16, jnp.float32
    dma = pltpu.SemaphoreType.DMA
    return pl.pallas_call(
        functools.partial(kernel, n_train, n_proj),
        out_shape=jax.ShapeDtypeStruct((STEPS, owned, QB), f32),
        in_specs=[
            pl.BlockSpec(memory_space=pl.ANY),
            pl.BlockSpec(memory_space=pl.ANY),
            pl.BlockSpec(memory_space=pltpu.VMEM),
            pl.BlockSpec(memory_space=pltpu.SMEM),
        ],
        out_specs=pl.BlockSpec(memory_space=pltpu.VMEM),
        scratch_shapes=[
            pltpu.VMEM((rows, width), bf16),
            [pltpu.VMEM((QBLK, CHUNK, width), bf16)] * NCHUNK,
            pltpu.VMEM((1, width), f32),
            pltpu.VMEM((STEPS - 1, QB, width), bf16),
            pltpu.VMEM((STEPS, QB, width), bf16),
            pltpu.VMEM((works, rows, 2 * CHUNK), bf16),
            pltpu.VMEM((works, owned, 2 * CHUNK), f32),
            pltpu.VMEM((works, n_proj - 1, owned, 2 * CHUNK), bf16),
            dma(()),
            dma((NCHUNK,)),
            dma((STEPS - 1, NCHUNK)),
            dma((STEPS - 1, NCHUNK)),
            dma((works, n_proj - 1)),
            dma((works, n_proj - 1)),
        ],
        compiler_params=pltpu.CompilerParams(
            collective_id=0, has_side_effects=True, vmem_limit_bytes=50 * 1024 * 1024
        ),
        cost_estimate=pl.CostEstimate(
            flops=2 * STEPS * rows * width * QB, bytes_accessed=2 * width * (rows + 512), transcendentals=width
        ),
    )(train_grads, queries.reshape(QBLK, QB, width), fisher.reshape(1, width), block_pick)


def solution(mesh):
    placed = (
        P(("groups", "train"), "proj"),
        P(("groups", "train"), "proj"),
        P(("groups", "proj")),
        P("groups", None),
    )
    return jax.shard_map(
        functools.partial(on_device, mesh.shape["train"], mesh.shape["proj"]),
        mesh=mesh,
        in_specs=placed,
        out_specs=P(None, ("groups", "train", "proj"), None),
        check_vma=False,
    )
```

time: 228 us -> 105 us (0.46)
  waiting for transfers between devices: 151 us -> 0 us
  Pallas kernels: 0 us -> 103 us
  matrix products: 29.5 us -> 0 us
  between operations: 21 us -> 0.01 us
  other arithmetic: 8.04 us -> 0 us
  starting transfers between devices: 7.97 us -> 0 us
  local copies, waits for them, and re-layouts: 9.71 us -> 2.37 us
    ppermute x3 -> x0, waiting for transfers between devices: 112 us -> none  [shifted(): lax.ppermute(array, axis, [(i, (i + by) % size) for i in range(size)])]
    pallas_call x0 -> x1, Pallas kernels: none -> 103 us  [on_device(): pl.pallas_call(functools.partial(kernel, n_train, n_proj), out_shape=jax....]
    reduce_scatter x4 -> x0, waiting for transfers between devices: 38.4 us -> none  [on_device(): lax.psum_scatter(lax.dot_general(train_grads, current, (((1,), (1,)), (()...]
    dot_general x4 -> x0, matrix products: 29.5 us -> none  [on_device(): lax.dot_general(train_grads, current, (((1,), (1,)), ((), ())), preferred...]
    ppermute x3 -> x0, starting transfers between devices: 7.66 us -> none  [shifted(): lax.ppermute(array, axis, [(i, (i + by) % size) for i in range(size)])]
    slice x3 -> x0, local copies, waits for them, and re-layouts: 4.87 us -> none  [the longest x2 4.28 us: on_device(): pending = pending[1:]]
    another operation x6 -> x0, other arithmetic: 4.77 us -> none  [the longest x5 3.96 us: on_device(): return jnp.stack(outputs)]
    convert_element_type x1 -> x0, other arithmetic: 3.27 us -> none  [on_device(): (queries.astype(jnp.float32) * lax.rsqrt(fisher)[None, :]).astype(jnp.bfl...]
  transfers between devices with their start and end apart: 7 -> 0, of which waited for: 5 -> 0; matrix products, arithmetic and copies ran while one was open for 15% -> 0% of each run, Pallas kernels for 0% -> 0%
where the time goes in v1:
time: 105 us
  Pallas kernels  103 us (98%)
  local copies, waits for them, and re-layouts  2.37 us (2%)
    pallas_call x1, Pallas kernels, on_device(): pl.pallas_call(functools.partial(kernel, n_train, n_proj), out_shape=jax....  103 us
    unnamed x5, local copies, waits for them, and re-layouts  2.37 us

profile of v1, /device:TPU:1, one launch (start us, length us, event | category | flops | bytes accessed | tf_op | source)
XLA Modules:
  0.0 104.9 jit_solution(5338896883403865241)
XLA Ops:
  0.0 0.0 copy-start
  0.0 0.7 copy-done
  0.7 0.0 copy-start.1
  0.7 0.7 copy-done.1
  1.4 102.6 %shard_map.46 = f32[4,256,256]{2,1,0:T(8,128)S(1)} custom-call(bf16[1024,4096]{1,0:T(8,128)(2,1)} %train_hbm.1, bf16[2,256,4096]{2,1,0:T(8,128)(2,1)} %bitcast.3, f32[1,4096]{1,0:T(1,128)S(1)} %bitcast.2, s32[4,4]{1,0:T(4,128)S(1)} %copy-done.1), custom_call_target="tpu_custom_call" | custom-call | flops 8589934592 | bytes 12582912 | tf_op jit(solution)/shard_map/pallas_call | solution.py:158
  104.0 1.0 copy.6
Async XLA Ops:
  0.0 0.7 copy-start
  0.7 0.7 copy-start.1

commit v2 on v1

v2 whole, which is shorter than its diff:
```python
import functools

import jax
import jax.numpy as jnp
from jax import lax
from jax.experimental import pallas as pl
from jax.experimental.pallas import tpu as pltpu
from jax.sharding import PartitionSpec as P

P_SIZE = 16384
QB = 256
QBLK = 2
STEPS = 4
LANES = 128
CHUNK = 64
NCHUNK = QB // CHUNK
FAR_ROWS = (32, 32, 64, 64, 32, 16, 16)
FAR_AT = tuple(sum(FAR_ROWS[:i]) for i in range(len(FAR_ROWS)))
FAR_CUTS = (1,) * (len(FAR_ROWS) - 1) + (2,)
NFAR = len(FAR_ROWS)
MAX_CUTS = max(FAR_CUTS)
MESH = pl.DeviceIdType.MESH


def fold_of(count):
    return LANES // (2 * count)


def kernel(
    n_train, n_proj, train_hbm, pool_hbm, fisher_hbm, pick_hbm, out,
    train, pools, fisher, inv_root, pick, far_out, near_out, near_blocks, far_blocks,
    partials, owns, landed, early,
    train_sem, pool_sem, small_sem, fsend_sem, frecv_sem, nsend_sem, nrecv_sem, zsend_sem, zrecv_sem,
):
    here, z = lax.axis_index("train"), lax.axis_index("proj")
    core = lax.rem(here, 2)
    rows, width = train.shape
    owned = rows // n_proj
    scale = P_SIZE ** (-0.5)

    barrier = pltpu.get_barrier_semaphore()
    for d in range(1, n_proj):
        pl.semaphore_signal(
            barrier, inc=1, device_id={"proj": lax.rem(z - d + n_proj, n_proj)}, device_id_type=MESH
        )
    for step in range(1, STEPS):
        source = lax.rem(here - step + n_train, n_train)
        pl.semaphore_signal(barrier, inc=1, device_id={"train": source}, device_id_type=MESH)
    pick_copy = pltpu.make_async_copy(pick_hbm, pick, small_sem.at[0])
    pick_copy.start()
    fisher_copy = pltpu.make_async_copy(fisher_hbm, fisher, small_sem.at[1])
    fisher_copy.start()
    pool_copies = []
    for c in range(NCHUNK):
        part = pl.ds(c * CHUNK, CHUNK)
        copy = pltpu.make_async_copy(pool_hbm.at[:, part], pools[c], pool_sem.at[c])
        copy.start()
        pool_copies.append(copy)
    train_copy = pltpu.make_async_copy(train_hbm, train, train_sem)
    train_copy.start()

    def far_copy(j, slot, p, cut):
        count, at = FAR_ROWS[p], FAR_AT[p]
        lanes = pl.ds(cut * (width // FAR_CUTS[p]), width // FAR_CUTS[p])
        return pltpu.make_async_remote_copy(
            src_ref=far_out.at[j, pl.ds(at, count), lanes],
            dst_ref=far_blocks[p].at[pl.ds(pl.multiple_of(slot * count, 16), count), lanes],
            send_sem=fsend_sem.at[j, p, cut],
            recv_sem=frecv_sem.at[slot, p, cut],
            device_id={"train": lax.rem(here + 2 - core + j, n_train)},
            device_id_type=MESH,
        )

    def near_copy(c):
        return pltpu.make_async_remote_copy(
            src_ref=near_out.at[pl.ds(c * CHUNK, CHUNK)],
            dst_ref=near_blocks[c].at[pl.ds(CHUNK, CHUNK)],
            send_sem=nsend_sem.at[c],
            recv_sem=nrecv_sem.at[c],
            device_id={"train": lax.rem(here + 1 + 2 * core, n_train)},
            device_id_type=MESH,
        )

    def condition(step, at, count, write):
        chosen = pick[step, here]
        piece = min(width, 512)
        c, first = at // CHUNK, at % CHUNK

        def body(i, _):
            part = pl.ds(pl.multiple_of(first + i * 16, 16), 16)
            for lane in range(0, width, piece):
                lanes = pl.ds(lane, piece)
                value = pools[c][chosen, part, lanes].astype(jnp.float32) * inv_root[:, lanes]
                write(pl.multiple_of(i * 16, 16), lanes, value.astype(jnp.bfloat16))
            return 0

        lax.fori_loop(0, count // 16, body, 0)

    pick_copy.wait()
    fisher_copy.wait()
    inv_root[...] = lax.rsqrt(fisher[...])
    entered = False
    for c in range(NCHUNK):
        pool_copies[c].wait()
        for p in range(NFAR):
            count, at = FAR_ROWS[p], FAR_AT[p]
            if at // CHUNK != c:
                continue
            for j in range(2):
                def write(i, lanes, value):
                    far_out[j, pl.ds(pl.multiple_of(at + i, 16), 16), lanes] = value

                condition(2 - core + j, at, count, write)
                if not entered:
                    pl.semaphore_wait(barrier, STEPS - 1 + n_proj - 1)
                    entered = True
                if FAR_CUTS[p] == 1:
                    far_copy(j, 1 - core, p, 0).start()
            if FAR_CUTS[p] > 1:
                for cut in range(FAR_CUTS[p]):
                    for j in range(2):
                        far_copy(j, 1 - core, p, cut).start()

        def write(i, lanes, value):
            near_out[pl.ds(pl.multiple_of(c * CHUNK + i, 16), 16), lanes] = value

        condition(1 + 2 * core, c * CHUNK, CHUNK, write)
        near_copy(c).start()
    for c in range(NCHUNK):
        def write(i, lanes, value):
            near_blocks[c][pl.ds(i, 16), lanes] = value

        condition(0, c * CHUNK, CHUNK, write)
    train_copy.wait()

    def partial_copy(k, d):
        to = lax.rem(z + d, n_proj)
        return pltpu.make_async_remote_copy(
            src_ref=partials[k].at[d - 1],
            dst_ref=landed[k].at[d - 1],
            send_sem=zsend_sem.at[k, d - 1],
            recv_sem=zrecv_sem.at[k, d - 1],
            device_id={"proj": to},
            device_id_type=MESH,
        )

    def finish(k, streams, count, at):
        fold = fold_of(count)
        share = owned // fold

        def add(d, total):
            partial_copy(k, d).wait_recv()
            return total + landed[k][d - 1].astype(jnp.float32)

        total = lax.fori_loop(1, n_proj, add, owns[k][...]) * scale
        for g in range(fold):
            for i, step in enumerate(streams):
                lane = g * 2 * count + i * count
                out[step, g * share:(g + 1) * share, at:at + count] = total[:, lane:lane + count]

    def dot(left, right):
        return lax.dot_general(left, right, (((1,), (1,)), ((), ())), preferred_element_type=jnp.float32)

    def mine(d):
        return pl.ds(pl.multiple_of(lax.rem(z + d, n_proj) * owned, 16), owned)

    near_in = 3 - 2 * core
    far_in = (1 + core, 2 + core)
    work = [((0, near_in), CHUNK, c * CHUNK, c, 1) for c in range(NCHUNK)]
    work += [(far_in, FAR_ROWS[p], FAR_AT[p], p, FAR_CUTS[p]) for p in range(NFAR)]
    for k, (streams, count, at, index, cuts) in enumerate(work):
        near = k < NCHUNK
        block = near_blocks[index] if near else far_blocks[index]
        fold = fold_of(count)
        share = owned // fold
        for cut in range(cuts):
            if near:
                near_copy(index).wait_recv()
            else:
                for slot in range(2):
                    far_copy(0, slot, index, cut).wait_recv()
            lanes = slice(cut * (width // cuts), (cut + 1) * (width // cuts))
            if cut < cuts - 1:
                def gather(d, _):
                    sums = dot(train[mine(d), lanes], block[:, lanes])
                    early[d - 1] = sums if cut == 0 else early[d - 1] + sums
                    return 0

                lax.fori_loop(1, n_proj + 1, gather, 0)
                continue

            def multiply(d, _):
                sums = dot(train[mine(d), lanes], block[:, lanes])
                if cuts > 1:
                    sums = sums + early[d - 1]
                if fold > 1:
                    sums = jnp.concatenate([sums[g * share:(g + 1) * share] for g in range(fold)], axis=1)

                @pl.when(d < n_proj)
                def _():
                    partials[k][d - 1] = sums.astype(jnp.bfloat16)
                    partial_copy(k, d).start()

                @pl.when(d == n_proj)
                def _():
                    owns[k][...] = sums

                return 0

            lax.fori_loop(1, n_proj + 1, multiply, 0)
        if k > 0:
            finish(k - 1, *work[k - 1][:3])
    finish(len(work) - 1, *work[-1][:3])

    for j in range(2):
        for p in range(NFAR):
            for cut in range(FAR_CUTS[p]):
                far_copy(j, 1 - core, p, cut).wait_send()
    for c in range(NCHUNK):
        near_copy(c).wait_send()
    for k in range(len(work)):
        def drain(d, _):
            partial_copy(k, d).wait_send()
            return 0

        lax.fori_loop(1, n_proj, drain, 0)


def on_device(n_train, n_proj, train_grads, queries, fisher, block_pick):
    rows, width = train_grads.shape
    owned = rows // n_proj
    counts = (CHUNK,) * NCHUNK + FAR_ROWS
    works = len(counts)
    bf16, f32 = jnp.bfloat16, jnp.float32
    dma = pltpu.SemaphoreType.DMA
    shares = [owned // fold_of(count) for count in counts]
    return pl.pallas_call(
        functools.partial(kernel, n_train, n_proj),
        out_shape=jax.ShapeDtypeStruct((STEPS, owned, QB), f32),
        in_specs=[pl.BlockSpec(memory_space=pl.ANY)] * 4,
        out_specs=pl.BlockSpec(memory_space=pltpu.VMEM),
        scratch_shapes=[
            pltpu.VMEM((rows, width), bf16),
            [pltpu.VMEM((QBLK, CHUNK, width), bf16)] * NCHUNK,
            pltpu.VMEM((1, width), f32),
            pltpu.VMEM((1, width), f32),
            pltpu.SMEM(block_pick.shape, jnp.int32),
            pltpu.VMEM((2, QB, width), bf16),
            pltpu.VMEM((QB, width), bf16),
            [pltpu.VMEM((2 * CHUNK, width), bf16)] * NCHUNK,
            [pltpu.VMEM((2 * count, width), bf16) for count in FAR_ROWS],
            [pltpu.VMEM((n_proj - 1, share, LANES), bf16) for share in shares],
            [pltpu.VMEM((share, LANES), f32) for share in shares],
            [pltpu.VMEM((n_proj - 1, share, LANES), bf16) for share in shares],
            pltpu.VMEM((n_proj, owned, 2 * FAR_ROWS[-1]), f32),
            dma(()),
            dma((NCHUNK,)),
            dma((2,)),
            dma((2, NFAR, MAX_CUTS)),
            dma((2, NFAR, MAX_CUTS)),
            dma((NCHUNK,)),
            dma((NCHUNK,)),
            dma((works, n_proj - 1)),
            dma((works, n_proj - 1)),
        ],
        compiler_params=pltpu.CompilerParams(
            collective_id=0, has_side_effects=True, vmem_limit_bytes=50 * 1024 * 1024
        ),
        cost_estimate=pl.CostEstimate(
            flops=2 * STEPS * rows * width * QB, bytes_accessed=2 * width * (rows + 512), transcendentals=width
        ),
    )(train_grads, queries.reshape(QBLK, QB, width), fisher.reshape(1, width), block_pick)


def solution(mesh):
    placed = (
        P(("groups", "train"), "proj"),
        P(("groups", "train"), "proj"),
        P(("groups", "proj")),
        P("groups", None),
    )
    return jax.shard_map(
        functools.partial(on_device, mesh.shape["train"], mesh.shape["proj"]),
        mesh=mesh,
        in_specs=placed,
        out_specs=P(None, ("groups", "train", "proj"), None),
        check_vma=False,
    )
```

time: 105 us -> 105 us (level)
  no operation moved by 1% of the time
where the time goes in v2:
time: 105 us; the launch traced here: 104 us
  Pallas kernels  102 us (97%)
  local copies, waits for them, and re-layouts  2.37 us (2%)
    pallas_call x1, Pallas kernels, on_device(): pl.pallas_call(functools.partial(kernel, n_train, n_proj), out_shape=jax....  102 us
    unnamed x5, local copies, waits for them, and re-layouts  2.37 us

profile of v2, /device:TPU:1, one launch (start us, length us, event | category | flops | bytes accessed | tf_op | source)
XLA Modules:
  0.0 104.0 jit_solution(615363191012360934)
XLA Ops:
  0.0 0.0 copy-start
  0.0 0.7 copy-done
  0.7 0.0 copy-start.1
  0.7 0.7 copy-done.1
  1.4 101.6 %shard_map.46 = f32[4,256,256]{2,1,0:T(8,128)S(1)} custom-call(bf16[1024,4096]{1,0:T(8,128)(2,1)} %train_hbm.1, bf16[2,256,4096]{2,1,0:T(8,128)(2,1)} %bitcast.3, f32[1,4096]{1,0:T(1,128)S(1)} %bitcast.2, s32[4,4]{1,0:T(4,128)S(1)} %copy-done.1), custom_call_target="tpu_custom_call" | custom-call | flops 8589934592 | bytes 12582912 | tf_op jit(solution)/shard_map/pallas_call | solution.py:237
  103.0 1.0 copy.6
Async XLA Ops:
  0.0 0.7 copy-start
  0.7 0.7 copy-start.1

commit v3 on v2

--- a/solution.py
+++ b/solution.py
@@ -30,7 +30,7 @@
     n_train, n_proj, train_hbm, pool_hbm, fisher_hbm, pick_hbm, out,
     train, pools, fisher, inv_root, pick, far_out, near_out, near_blocks, far_blocks,
     partials, owns, landed, early,
-    train_sem, pool_sem, small_sem, fsend_sem, frecv_sem, nsend_sem, nrecv_sem, zsend_sem, zrecv_sem,
+    inside, train_sem, pool_sem, small_sem, fsend_sem, frecv_sem, nsend_sem, nrecv_sem, zsend_sem, zrecv_sem,
 ):
     here, z = lax.axis_index("train"), lax.axis_index("proj")
     core = lax.rem(here, 2)
@@ -39,13 +39,15 @@
     scale = P_SIZE ** (-0.5)
 
     barrier = pltpu.get_barrier_semaphore()
-    for d in range(1, n_proj):
-        pl.semaphore_signal(
-            barrier, inc=1, device_id={"proj": lax.rem(z - d + n_proj, n_proj)}, device_id_type=MESH
-        )
+    for other in (z - 1, z + 1):
+        @pl.when(jnp.logical_and(other >= 0, other < n_proj))
+        def _():
+            pl.semaphore_signal(barrier, inc=1, device_id={"proj": other}, device_id_type=MESH)
+
     for step in range(1, STEPS):
         source = lax.rem(here - step + n_train, n_train)
         pl.semaphore_signal(barrier, inc=1, device_id={"train": source}, device_id_type=MESH)
+    beside = jnp.where(z > 0, 1, 0) + jnp.where(z < n_proj - 1, 1, 0)
     pick_copy = pltpu.make_async_copy(pick_hbm, pick, small_sem.at[0])
     pick_copy.start()
     fisher_copy = pltpu.make_async_copy(fisher_hbm, fisher, small_sem.at[1])
@@ -54,10 +56,9 @@
     for c in range(NCHUNK):
         part = pl.ds(c * CHUNK, CHUNK)
         copy = pltpu.make_async_copy(pool_hbm.at[:, part], pools[c], pool_sem.at[c])
-        copy.start()
+        if c == 0:
+            copy.start()
         pool_copies.append(copy)
-    train_copy = pltpu.make_async_copy(train_hbm, train, train_sem)
-    train_copy.start()
 
     def far_copy(j, slot, p, cut):
         count, at = FAR_ROWS[p], FAR_AT[p]
@@ -112,7 +113,7 @@
 
                 condition(2 - core + j, at, count, write)
                 if not entered:
-                    pl.semaphore_wait(barrier, STEPS - 1 + n_proj - 1)
+                    pl.semaphore_wait(barrier, STEPS - 1 + beside)
                     entered = True
                 if FAR_CUTS[p] == 1:
                     far_copy(j, 1 - core, p, 0).start()
@@ -124,14 +125,37 @@
         def write(i, lanes, value):
             near_out[pl.ds(pl.multiple_of(c * CHUNK + i, 16), 16), lanes] = value
 
+        if c == 0:
+            for copy in pool_copies[1:]:
+                copy.start()
         condition(1 + 2 * core, c * CHUNK, CHUNK, write)
         near_copy(c).start()
+        if c == 0:
+            train_copy = pltpu.make_async_copy(train_hbm, train, train_sem)
+            train_copy.start()
     for c in range(NCHUNK):
         def write(i, lanes, value):
             near_blocks[c][pl.ds(i, 16), lanes] = value
 
         condition(0, c * CHUNK, CHUNK, write)
     train_copy.wait()
+
+    def relay(i, _):
+        for origin, onward in ((z - i, z + 1), (z + i, z - 1)):
+            known = jnp.logical_and(origin >= 0, origin < n_proj)
+
+            @pl.when(jnp.logical_and(known, i > 1))
+            def _():
+                pl.semaphore_wait(inside.at[origin], 1)
+
+            @pl.when(jnp.logical_and(known, jnp.logical_and(onward >= 0, onward < n_proj)))
+            def _():
+                pl.semaphore_signal(
+                    inside.at[origin], inc=1, device_id={"proj": onward}, device_id_type=MESH
+                )
+        return 0
+
+    lax.fori_loop(1, n_proj, relay, 0)
 
     def partial_copy(k, d):
         to = lax.rem(z + d, n_proj)
@@ -164,6 +188,18 @@
     def mine(d):
         return pl.ds(pl.multiple_of(lax.rem(z + d, n_proj) * owned, 16), owned)
 
+    def drain_far(p):
+        for j in range(2):
+            for cut in range(FAR_CUTS[p]):
+                far_copy(j, 1 - core, p, cut).wait_send()
+
+    def drain_partial(k):
+        def drain(d, _):
+            partial_copy(k, d).wait_send()
+            return 0
+
+        lax.fori_loop(1, n_proj, drain, 0)
+
     near_in = 3 - 2 * core
     far_in = (1 + core, 2 + core)
     work = [((0, near_in), CHUNK, c * CHUNK, c, 1) for c in range(NCHUNK)]
@@ -174,6 +210,15 @@
         fold = fold_of(count)
         share = owned // fold
         for cut in range(cuts):
+            if k > NCHUNK and cut == cuts - 1:
+                finish(k - 1, *work[k - 1][:3])
+            if k == len(work) - 1 and cut == cuts - 1:
+                for p in range(NFAR - 1):
+                    drain_far(p)
+                for c in range(NCHUNK):
+                    near_copy(c).wait_send()
+                for before in range(k):
+                    drain_partial(before)
             if near:
                 near_copy(index).wait_recv()
             else:
@@ -208,22 +253,12 @@
                 return 0
 
             lax.fori_loop(1, n_proj + 1, multiply, 0)
-        if k > 0:
+        if 0 < k <= NCHUNK:
             finish(k - 1, *work[k - 1][:3])
     finish(len(work) - 1, *work[-1][:3])
 
-    for j in range(2):
-        for p in range(NFAR):
-            for cut in range(FAR_CUTS[p]):
-                far_copy(j, 1 - core, p, cut).wait_send()
-    for c in range(NCHUNK):
-        near_copy(c).wait_send()
-    for k in range(len(work)):
-        def drain(d, _):
-            partial_copy(k, d).wait_send()
-            return 0
-
-        lax.fori_loop(1, n_proj, drain, 0)
+    drain_far(NFAR - 1)
+    drain_partial(len(work) - 1)
 
 
 def on_device(n_train, n_proj, train_grads, queries, fisher, block_pick):
@@ -253,6 +288,7 @@
             [pltpu.VMEM((share, LANES), f32) for share in shares],
             [pltpu.VMEM((n_proj - 1, share, LANES), bf16) for share in shares],
             pltpu.VMEM((n_proj, owned, 2 * FAR_ROWS[-1]), f32),
+            pltpu.SemaphoreType.REGULAR((n_proj,)),
             dma(()),
             dma((NCHUNK,)),
             dma((2,)),

time: 105 us -> 104 us (level)
  no operation moved by 1% of the time
where the time goes in v3:
time: 104 us
  Pallas kernels  102 us (98%)
  local copies, waits for them, and re-layouts  2.37 us (2%)
    pallas_call x1, Pallas kernels, on_device(): pl.pallas_call(functools.partial(kernel, n_train, n_proj), out_shape=jax....  102 us
    unnamed x5, local copies, waits for them, and re-layouts  2.37 us

profile of v3, /device:TPU:1, one launch (start us, length us, event | category | flops | bytes accessed | tf_op | source)
XLA Modules:
  0.0 103.9 jit_solution(9408254133142768590)
XLA Ops:
  0.0 0.0 copy-start
  0.0 0.7 copy-done
  0.7 0.0 copy-start.1
  0.7 0.7 copy-done.1
  1.4 101.5 %shard_map.46 = f32[4,256,256]{2,1,0:T(8,128)S(1)} custom-call(bf16[1024,4096]{1,0:T(8,128)(2,1)} %train_hbm.1, bf16[2,256,4096]{2,1,0:T(8,128)(2,1)} %bitcast.3, f32[1,4096]{1,0:T(1,128)S(1)} %bitcast.2, s32[4,4]{1,0:T(4,128)S(1)} %copy-done.1), custom_call_target="tpu_custom_call" | custom-call | flops 8589934592 | bytes 12582912 | tf_op jit(solution)/shard_map/pallas_call | solution.py:272
  102.9 1.0 copy.6
Async XLA Ops:
  0.0 0.7 copy-start
  0.7 0.7 copy-start.1
